TPU v7x, 128 devices: a whole 4x4x4 slice. The times are simulated.
128 devices in a mesh: seq: 128 (over y, x, z, core).
Axes of the slice: x: 4, y: 4, z: 4, core: 2. Of those that a mesh axis runs over, the one named last changes fastest.
Arguments:
- queries: bfloat16 [524288, 768], P('seq'), may hold values from -8 to 8
- key_rows: bfloat16 [524288, 768], P('seq'), may hold values from -8 to 8
- value_rows: bfloat16 [524288, 768], P('seq'), may hold values from -6 to 6
Outputs:
- mixed: bfloat16 [524288, 768], P('seq')
All inputs are finite; a program needn't handle non-finite values.
Results may differ from a plain program's by a relative error of at most 0.0037.
Values may be sent and summed in bfloat16 or wider, within the bound.
No kernel may reach another device: no remote copies, remote signals or barrier semaphores. Data moves between devices by JAX's collectives and lax.ppermute only.
A program may use at most 128 MiB of HBM per device.

v0:
```python
import jax
import jax.numpy as jnp
from jax import lax
from jax.sharding import PartitionSpec as P

HEADS = 12
BLOCK = 512
KEEP = 512


masked_score = -1e30


def column_owner(width, head_count):
    head_size = width // head_count
    owner = jnp.arange(width, dtype=jnp.int32) // head_size
    return owner[None, :] == jnp.arange(head_count, dtype=jnp.int32)[:, None]


def pick_rows(array, stride, head_count):
    rows, width = array.shape
    corner = array.reshape(rows // stride, stride, width)[:, :head_count]
    owned = column_owner(width, head_count)
    chosen = jnp.where(owned[None], corner.astype(jnp.float32), 0.0)
    return jnp.sum(chosen, axis=1)


def pick_lse(lse_rows, stride, head_count):
    tokens = lse_rows.shape[1]
    corner = lse_rows.reshape(head_count, tokens // stride, stride)[:, :, :head_count]
    diagonal_mask = jnp.eye(head_count, dtype=bool)[:, None, :]
    return jnp.transpose(jnp.sum(jnp.where(diagonal_mask, corner, 0.0), axis=2))


def put_rows(complete, merged, stride, head_count):
    rows, width = complete.shape
    shaped = complete.reshape(rows // stride, stride, width)
    owned = column_owner(width, head_count)
    corner = jnp.where(owned[None], merged[:, None, :], shaped[:, :head_count])
    shaped = lax.dynamic_update_slice(shaped, corner, (0, 0, 0))
    return shaped.reshape(rows, width)


def attend_core(query_set, key_set, value_set, query_place, key_place):
    factor = query_set.shape[-1] ** (-0.5)
    scores = (
        jnp.einsum("qhe,khe->hqk", query_set, key_set, preferred_element_type=jnp.float32) * factor
    )
    scores = jnp.where(key_place[None, None, :] <= query_place[None, :, None], scores, masked_score)
    highest = jnp.max(scores, axis=-1)
    expanded = jnp.exp(scores - highest[..., None])
    totals = jnp.sum(expanded, axis=-1)
    probs = expanded.astype(jnp.bfloat16)
    result = jnp.einsum("hqk,khe->qhe", probs, value_set, preferred_element_type=jnp.float32)
    result = result / jnp.transpose(totals)[..., None]
    return (result, highest + jnp.log(totals))


def combine(out_zero, lse_zero, out_one, lse_one, out_two, lse_two, out_three, lse_three):
    row_ids = jnp.arange(out_zero.shape[0], dtype=jnp.int32)
    inside_two = (row_ids % 2 == 0)[:, None]
    inside_three = (row_ids % 4 == 0)[:, None]
    highest = jnp.maximum(lse_zero, lse_one)
    highest = jnp.where(inside_two, jnp.maximum(highest, lse_two), highest)
    highest = jnp.where(inside_three, jnp.maximum(highest, lse_three), highest)
    weight_zero = jnp.exp(lse_zero - highest)
    weight_one = jnp.exp(lse_one - highest)
    weight_two = jnp.where(inside_two, jnp.exp(lse_two - highest), 0.0)
    weight_three = jnp.where(inside_three, jnp.exp(lse_three - highest), 0.0)
    summed = weight_zero[..., None] * out_zero + weight_one[..., None] * out_one
    summed = summed + weight_two[..., None] * out_two + weight_three[..., None] * out_three
    return summed / (weight_zero + weight_one + weight_two + weight_three)[..., None]


def local(queries, key_rows, value_rows):
    tokens, model_width = queries.shape
    head_count = HEADS
    head_size = model_width // head_count
    devices = lax.axis_size("seq")
    device = lax.axis_index("seq")
    rows_one = 4 * KEEP // devices
    stride = tokens // rows_one
    query_one = pick_rows(queries, stride, head_count).astype(jnp.bfloat16)
    key_one = pick_rows(key_rows, stride, head_count).astype(jnp.bfloat16)
    value_one = pick_rows(value_rows, stride, head_count).astype(jnp.bfloat16)
    packed = jnp.concatenate([key_one, value_one], 1)
    quarter = devices // 4
    gathered = lax.all_gather(packed, "seq", axis=0, tiled=True)
    first_level = lax.dynamic_slice_in_dim(gathered, device // quarter * KEEP, KEEP, 0)
    half_rows = lax.dynamic_slice_in_dim(
        gathered, device // (2 * quarter) * (2 * KEEP), 2 * KEEP, 0
    )
    second_level = half_rows[::2]
    third_level = gathered[::4]
    blocks = tokens // BLOCK
    places = jnp.arange(BLOCK, dtype=jnp.int32)
    shape_heads = (BLOCK, head_count, head_size)

    def local_block(triple):
        result, lse_rows = attend_core(
            triple[0].reshape(shape_heads),
            triple[1].reshape(shape_heads),
            triple[2].reshape(shape_heads),
            places,
            places,
        )
        return (result.reshape(BLOCK, model_width), lse_rows)

    shape_blocks = (blocks, BLOCK, model_width)
    out_zero, lse_zero = lax.map(
        local_block,
        (
            queries.reshape(shape_blocks),
            key_rows.reshape(shape_blocks),
            value_rows.reshape(shape_blocks),
        ),
    )
    out_zero = out_zero.reshape(tokens, model_width)
    lse_zero = jnp.moveaxis(lse_zero, 0, 1).reshape(head_count, tokens)
    keep_places = jnp.arange(KEEP, dtype=jnp.int32)

    def level(collected, query_set, query_start):
        key_set = collected[:, :model_width].reshape(KEEP, head_count, head_size)
        value_set = collected[:, model_width:].reshape(KEEP, head_count, head_size)
        query_place = query_start + jnp.arange(query_set.shape[0], dtype=jnp.int32)
        query_split = query_set.reshape(query_set.shape[0], head_count, head_size)
        result, lse_rows = attend_core(query_split, key_set, value_set, query_place, keep_places)
        return (result, jnp.transpose(lse_rows))

    out_one, lse_one = level(first_level, query_one, device % quarter * rows_one)
    out_two, lse_two = level(second_level, query_one[::2], device % (2 * quarter) * (rows_one // 2))
    out_three, lse_three = level(third_level, query_one[::4], device * (rows_one // 4))
    picked_out = pick_rows(out_zero, stride, head_count).reshape(rows_one, head_count, head_size)
    picked_lse = pick_lse(lse_zero, stride, head_count)
    merged = combine(
        picked_out,
        picked_lse,
        out_one,
        lse_one,
        jnp.repeat(out_two, 2, axis=0),
        jnp.repeat(lse_two, 2, axis=0),
        jnp.repeat(out_three, 4, axis=0),
        jnp.repeat(lse_three, 4, axis=0),
    )
    return put_rows(out_zero, merged.reshape(rows_one, model_width), stride, head_count).astype(
        jnp.bfloat16
    )


def solution(mesh):
    in_specs = (P("seq", None), P("seq", None), P("seq", None))
    out_specs = P("seq", None)
    return jax.shard_map(local, mesh=mesh, in_specs=in_specs, out_specs=out_specs, check_vma=False)
```

profile of v0, /device:TPU:1, one launch (start us, length us, event | category | flops | bytes accessed | tf_op | source)
XLA Modules:
  0.0 253.5 jit_solution(9391518833948652428)
XLA Ops:
  6.5 113.8 %while.13 = (s32[]{:T(128)}, f32[8,512,768]{2,1,0:T(8,128)}, f32[8,12,512]{2,1,0:T(8,128)S(1)}, bf16[8,512,768]{2,1,0:T(8,128)(2,1)}, bf16[8,512,768]{2,1,0:T(8,...) while((s32[]{:T(128)}, f32[8,512,768]{2,1,0:T(8,128)}, f32[8,12,512]{2,1,0:T(8,128)S(1)}, ...), condition=%wide.region_3.4_spmd.clone, body=%wide.region_0.3_spmd.clone.sunk | while | flops 840558592 | bytes 61825152 | solution.py:110
  13.1 2.6 %fusion.71 = f32[12,512]{1,0:T(8,128)S(1)} fusion(f32[12,512,512]{1,2,0:T(8,128)S(1)} %get-tuple-element.153, f32[12,512]{1,0:T(8,128)S(1)} %get-tuple-element.154, pred[512,512]{0,1:T(8,128)(4,1)S(1)} %iota_compare_fusion.7), kind=kLoop, calls=%fused_computation.4.clone.1 | loop fusion | flops 12576768 | bytes 12894208 | tf_op jit(solution)/shard_map/while/body/eval_jaxpr/reduce_sum | solution.py:52
  15.7 3.3 %bitcast_divide_fusion.2 = f32[512,12,64]{0,2,1:T(8,128)S(1)} fusion(bf16[512,12,64]{0,2,1:T(8,128)(2,1)S(1)} %bitcast.109, f32[12,512,512]{1,2,0:T(8,128)S(1)} %get-tuple-element.153, f32[12,512]{1,0:T(8,128)S(1)} %get-tuple-element.154, pred[512,512]{0,1:T(8,128)(4,1)S(1)} %iota_compare_fusion.7, f32[512,12]{0,1:T(8,128)S(1)} %bitcast.113), kind=kOutput, calls=%fused_computation.8.clone.1 | convolution fusion | flops 415629312 | bytes 15253504 | tf_op jit(solution)/shard_map/while/body/eval_jaxpr/hqk,khe->qhe/dot_general | solution.py:54
  27.3 2.6 %fusion.71 = f32[12,512]{1,0:T(8,128)S(1)} fusion(f32[12,512,512]{1,2,0:T(8,128)S(1)} %get-tuple-element.153, f32[12,512]{1,0:T(8,128)S(1)} %get-tuple-element.154, pred[512,512]{0,1:T(8,128)(4,1)S(1)} %iota_compare_fusion.7), kind=kLoop, calls=%fused_computation.4.clone.1 | loop fusion | flops 12576768 | bytes 12894208 | tf_op jit(solution)/shard_map/while/body/eval_jaxpr/reduce_sum | solution.py:52
  29.9 3.3 %bitcast_divide_fusion.2 = f32[512,12,64]{0,2,1:T(8,128)S(1)} fusion(bf16[512,12,64]{0,2,1:T(8,128)(2,1)S(1)} %bitcast.109, f32[12,512,512]{1,2,0:T(8,128)S(1)} %get-tuple-element.153, f32[12,512]{1,0:T(8,128)S(1)} %get-tuple-element.154, pred[512,512]{0,1:T(8,128)(4,1)S(1)} %iota_compare_fusion.7, f32[512,12]{0,1:T(8,128)S(1)} %bitcast.113), kind=kOutput, calls=%fused_computation.8.clone.1 | convolution fusion | flops 415629312 | bytes 15253504 | tf_op jit(solution)/shard_map/while/body/eval_jaxpr/hqk,khe->qhe/dot_general | solution.py:54
  41.5 2.6 %fusion.71 = f32[12,512]{1,0:T(8,128)S(1)} fusion(f32[12,512,512]{1,2,0:T(8,128)S(1)} %get-tuple-element.153, f32[12,512]{1,0:T(8,128)S(1)} %get-tuple-element.154, pred[512,512]{0,1:T(8,128)(4,1)S(1)} %iota_compare_fusion.7), kind=kLoop, calls=%fused_computation.4.clone.1 | loop fusion | flops 12576768 | bytes 12894208 | tf_op jit(solution)/shard_map/while/body/eval_jaxpr/reduce_sum | solution.py:52
  44.1 3.3 %bitcast_divide_fusion.2 = f32[512,12,64]{0,2,1:T(8,128)S(1)} fusion(bf16[512,12,64]{0,2,1:T(8,128)(2,1)S(1)} %bitcast.109, f32[12,512,512]{1,2,0:T(8,128)S(1)} %get-tuple-element.153, f32[12,512]{1,0:T(8,128)S(1)} %get-tuple-element.154, pred[512,512]{0,1:T(8,128)(4,1)S(1)} %iota_compare_fusion.7, f32[512,12]{0,1:T(8,128)S(1)} %bitcast.113), kind=kOutput, calls=%fused_computation.8.clone.1 | convolution fusion | flops 415629312 | bytes 15253504 | tf_op jit(solution)/shard_map/while/body/eval_jaxpr/hqk,khe->qhe/dot_general | solution.py:54
  55.7 2.6 %fusion.71 = f32[12,512]{1,0:T(8,128)S(1)} fusion(f32[12,512,512]{1,2,0:T(8,128)S(1)} %get-tuple-element.153, f32[12,512]{1,0:T(8,128)S(1)} %get-tuple-element.154, pred[512,512]{0,1:T(8,128)(4,1)S(1)} %iota_compare_fusion.7), kind=kLoop, calls=%fused_computation.4.clone.1 | loop fusion | flops 12576768 | bytes 12894208 | tf_op jit(solution)/shard_map/while/body/eval_jaxpr/reduce_sum | solution.py:52
  58.3 3.3 %bitcast_divide_fusion.2 = f32[512,12,64]{0,2,1:T(8,128)S(1)} fusion(bf16[512,12,64]{0,2,1:T(8,128)(2,1)S(1)} %bitcast.109, f32[12,512,512]{1,2,0:T(8,128)S(1)} %get-tuple-element.153, f32[12,512]{1,0:T(8,128)S(1)} %get-tuple-element.154, pred[512,512]{0,1:T(8,128)(4,1)S(1)} %iota_compare_fusion.7, f32[512,12]{0,1:T(8,128)S(1)} %bitcast.113), kind=kOutput, calls=%fused_computation.8.clone.1 | convolution fusion | flops 415629312 | bytes 15253504 | tf_op jit(solution)/shard_map/while/body/eval_jaxpr/hqk,khe->qhe/dot_general | solution.py:54
  70.0 2.6 %fusion.71 = f32[12,512]{1,0:T(8,128)S(1)} fusion(f32[12,512,512]{1,2,0:T(8,128)S(1)} %get-tuple-element.153, f32[12,512]{1,0:T(8,128)S(1)} %get-tuple-element.154, pred[512,512]{0,1:T(8,128)(4,1)S(1)} %iota_compare_fusion.7), kind=kLoop, calls=%fused_computation.4.clone.1 | loop fusion | flops 12576768 | bytes 12894208 | tf_op jit(solution)/shard_map/while/body/eval_jaxpr/reduce_sum | solution.py:52
  72.6 3.3 %bitcast_divide_fusion.2 = f32[512,12,64]{0,2,1:T(8,128)S(1)} fusion(bf16[512,12,64]{0,2,1:T(8,128)(2,1)S(1)} %bitcast.109, f32[12,512,512]{1,2,0:T(8,128)S(1)} %get-tuple-element.153, f32[12,512]{1,0:T(8,128)S(1)} %get-tuple-element.154, pred[512,512]{0,1:T(8,128)(4,1)S(1)} %iota_compare_fusion.7, f32[512,12]{0,1:T(8,128)S(1)} %bitcast.113), kind=kOutput, calls=%fused_computation.8.clone.1 | convolution fusion | flops 415629312 | bytes 15253504 | tf_op jit(solution)/shard_map/while/body/eval_jaxpr/hqk,khe->qhe/dot_general | solution.py:54
  84.2 2.6 %fusion.71 = f32[12,512]{1,0:T(8,128)S(1)} fusion(f32[12,512,512]{1,2,0:T(8,128)S(1)} %get-tuple-element.153, f32[12,512]{1,0:T(8,128)S(1)} %get-tuple-element.154, pred[512,512]{0,1:T(8,128)(4,1)S(1)} %iota_compare_fusion.7), kind=kLoop, calls=%fused_computation.4.clone.1 | loop fusion | flops 12576768 | bytes 12894208 | tf_op jit(solution)/shard_map/while/body/eval_jaxpr/reduce_sum | solution.py:52
  86.8 3.3 %bitcast_divide_fusion.2 = f32[512,12,64]{0,2,1:T(8,128)S(1)} fusion(bf16[512,12,64]{0,2,1:T(8,128)(2,1)S(1)} %bitcast.109, f32[12,512,512]{1,2,0:T(8,128)S(1)} %get-tuple-element.153, f32[12,512]{1,0:T(8,128)S(1)} %get-tuple-element.154, pred[512,512]{0,1:T(8,128)(4,1)S(1)} %iota_compare_fusion.7, f32[512,12]{0,1:T(8,128)S(1)} %bitcast.113), kind=kOutput, calls=%fused_computation.8.clone.1 | convolution fusion | flops 415629312 | bytes 15253504 | tf_op jit(solution)/shard_map/while/body/eval_jaxpr/hqk,khe->qhe/dot_general | solution.py:54
  98.5 2.6 %fusion.71 = f32[12,512]{1,0:T(8,128)S(1)} fusion(f32[12,512,512]{1,2,0:T(8,128)S(1)} %get-tuple-element.153, f32[12,512]{1,0:T(8,128)S(1)} %get-tuple-element.154, pred[512,512]{0,1:T(8,128)(4,1)S(1)} %iota_compare_fusion.7), kind=kLoop, calls=%fused_computation.4.clone.1 | loop fusion | flops 12576768 | bytes 12894208 | tf_op jit(solution)/shard_map/while/body/eval_jaxpr/reduce_sum | solution.py:52
  101.1 3.3 %bitcast_divide_fusion.2 = f32[512,12,64]{0,2,1:T(8,128)S(1)} fusion(bf16[512,12,64]{0,2,1:T(8,128)(2,1)S(1)} %bitcast.109, f32[12,512,512]{1,2,0:T(8,128)S(1)} %get-tuple-element.153, f32[12,512]{1,0:T(8,128)S(1)} %get-tuple-element.154, pred[512,512]{0,1:T(8,128)(4,1)S(1)} %iota_compare_fusion.7, f32[512,12]{0,1:T(8,128)S(1)} %bitcast.113), kind=kOutput, calls=%fused_computation.8.clone.1 | convolution fusion | flops 415629312 | bytes 15253504 | tf_op jit(solution)/shard_map/while/body/eval_jaxpr/hqk,khe->qhe/dot_general | solution.py:54
  112.7 2.6 %fusion.71 = f32[12,512]{1,0:T(8,128)S(1)} fusion(f32[12,512,512]{1,2,0:T(8,128)S(1)} %get-tuple-element.153, f32[12,512]{1,0:T(8,128)S(1)} %get-tuple-element.154, pred[512,512]{0,1:T(8,128)(4,1)S(1)} %iota_compare_fusion.7), kind=kLoop, calls=%fused_computation.4.clone.1 | loop fusion | flops 12576768 | bytes 12894208 | tf_op jit(solution)/shard_map/while/body/eval_jaxpr/reduce_sum | solution.py:52
  115.3 3.3 %bitcast_divide_fusion.2 = f32[512,12,64]{0,2,1:T(8,128)S(1)} fusion(bf16[512,12,64]{0,2,1:T(8,128)(2,1)S(1)} %bitcast.109, f32[12,512,512]{1,2,0:T(8,128)S(1)} %get-tuple-element.153, f32[12,512]{1,0:T(8,128)S(1)} %get-tuple-element.154, pred[512,512]{0,1:T(8,128)(4,1)S(1)} %iota_compare_fusion.7, f32[512,12]{0,1:T(8,128)S(1)} %bitcast.113), kind=kOutput, calls=%fused_computation.8.clone.1 | convolution fusion | flops 415629312 | bytes 15253504 | tf_op jit(solution)/shard_map/while/body/eval_jaxpr/hqk,khe->qhe/dot_general | solution.py:54
  120.3 2.2 select_reduce_fusion
  124.9 70.3 %all-gather.2.cloned.1.call-done = bf16[2048,1536]{1,0:T(8,128)(2,1)} async-done(((bf16[16,1536]{1,0:T(8,128)(2,1)}), bf16[2048,1536]{1,0:T(8,128)(2,1)}) %all-gather.2.cloned.1.call-update) | async-done | bytes 6291472 | tf_op jit(solution)/shard_map/all_gather | solution.py:88
  199.0 12.3 %slice.55 = bf16[512,1536]{1,0:T(8,128)(2,1)S(1)} slice(bf16[2048,1536]{1,0:T(8,128)(2,1)} %all-gather.2.cloned.1.call-done), slice={[0:2048:4], [0:1536:1]} | slice | bytes 3145728 | tf_op jit(solution)/shard_map/slice | solution.py:94
  213.8 2.1 constant_dynamic-slice_fusion.4
  215.9 8.0 %slice.52 = bf16[512,1536]{1,0:T(8,128)(2,1)} slice(bf16[1024,1536]{1,0:T(8,128)(2,1)S(1)} %constant_dynamic-slice_fusion.4), slice={[0:1024:2], [0:1536:1]} | slice | bytes 3145728 | tf_op jit(solution)/shard_map/slice | solution.py:93
  233.8 4.7 %dynamic_update_slice.11 = f32[16,256,768]{2,1,0:T(8,128)} dynamic-update-slice(f32[16,256,768]{2,1,0:T(8,128)} %bitcast.112, f32[16,12,768]{2,1,0:T(8,128)S(1)} %slice_select_fusion, s32[]{:T(128)} %constant.117.clone.1, s32[]{:T(128)} %constant.117.clone.1, s32[]{:T(128)} %constant.117.clone.1) | dynamic-update-slice | bytes 1179652 | tf_op jit(solution)/shard_map/dynamic_update_slice | solution.py:40
  238.6 8.1 %convert_element_type.50 = bf16[16,256,768]{2,1,0:T(8,128)(2,1)} convert(f32[16,256,768]{2,1,0:T(8,128)} %dynamic_update_slice.11) | non-fusion elementwise | flops 3145728 | bytes 18874368 | tf_op jit(solution)/shard_map/convert_element_type | solution.py:145
  (156 shorter events, 84.7 us)
Async XLA Ops:
  6.5 188.6 %all-gather.2.cloned.1.call-start = ((), (), s32[]{:S(2)}) async-start(), calls=%async_computation | async-start | bytes 6340608 | tf_op jit(solution)/shard_map/all_gather | solution.py:88
  13.1 2.6 %copy-start = (bf16[1,512,768]{1,2,0:T(8,128)(2,1)S(1)}, bf16[1,512,768]{1,2,0:T(8,128)(2,1)}, u32[]{:S(2)}) copy-start(bf16[1,512,768]{1,2,0:T(8,128)(2,1)} %copy.81) | copy-start | bytes 2359300 | tf_op jit(solution)/shard_map/while
  27.3 2.6 %copy-start = (bf16[1,512,768]{1,2,0:T(8,128)(2,1)S(1)}, bf16[1,512,768]{1,2,0:T(8,128)(2,1)}, u32[]{:S(2)}) copy-start(bf16[1,512,768]{1,2,0:T(8,128)(2,1)} %copy.81) | copy-start | bytes 2359300 | tf_op jit(solution)/shard_map/while
  41.5 2.6 %copy-start = (bf16[1,512,768]{1,2,0:T(8,128)(2,1)S(1)}, bf16[1,512,768]{1,2,0:T(8,128)(2,1)}, u32[]{:S(2)}) copy-start(bf16[1,512,768]{1,2,0:T(8,128)(2,1)} %copy.81) | copy-start | bytes 2359300 | tf_op jit(solution)/shard_map/while
  55.7 2.6 %copy-start = (bf16[1,512,768]{1,2,0:T(8,128)(2,1)S(1)}, bf16[1,512,768]{1,2,0:T(8,128)(2,1)}, u32[]{:S(2)}) copy-start(bf16[1,512,768]{1,2,0:T(8,128)(2,1)} %copy.81) | copy-start | bytes 2359300 | tf_op jit(solution)/shard_map/while
  70.0 2.6 %copy-start = (bf16[1,512,768]{1,2,0:T(8,128)(2,1)S(1)}, bf16[1,512,768]{1,2,0:T(8,128)(2,1)}, u32[]{:S(2)}) copy-start(bf16[1,512,768]{1,2,0:T(8,128)(2,1)} %copy.81) | copy-start | bytes 2359300 | tf_op jit(solution)/shard_map/while
  84.2 2.6 %copy-start = (bf16[1,512,768]{1,2,0:T(8,128)(2,1)S(1)}, bf16[1,512,768]{1,2,0:T(8,128)(2,1)}, u32[]{:S(2)}) copy-start(bf16[1,512,768]{1,2,0:T(8,128)(2,1)} %copy.81) | copy-start | bytes 2359300 | tf_op jit(solution)/shard_map/while
  98.5 2.6 %copy-start = (bf16[1,512,768]{1,2,0:T(8,128)(2,1)S(1)}, bf16[1,512,768]{1,2,0:T(8,128)(2,1)}, u32[]{:S(2)}) copy-start(bf16[1,512,768]{1,2,0:T(8,128)(2,1)} %copy.81) | copy-start | bytes 2359300 | tf_op jit(solution)/shard_map/while
  112.7 2.6 %copy-start = (bf16[1,512,768]{1,2,0:T(8,128)(2,1)S(1)}, bf16[1,512,768]{1,2,0:T(8,128)(2,1)}, u32[]{:S(2)}) copy-start(bf16[1,512,768]{1,2,0:T(8,128)(2,1)} %copy.81) | copy-start | bytes 2359300 | tf_op jit(solution)/shard_map/while
  211.4 20.7 %copy-start.2 = (f32[16,12,64]{2,1,0:T(8,128)S(1)}, f32[16,12,64]{2,1,0:T(8,128)}, u32[]{:S(2)}) copy-start(f32[16,12,64]{2,1,0:T(8,128)} %reshape.292) | copy-start | bytes 147460
  223.8 8.3 %copy-start.1 = (bf16[512,768]{0,1:T(8,128)(2,1)S(1)}, bf16[512,768]{0,1:T(8,128)(2,1)}, u32[]{:S(2)}) copy-start(bf16[512,768]{0,1:T(8,128)(2,1)} %copy.42) | copy-start | bytes 2359300
Sparse Core Ops, SparseCore 0:
  123.3 71.8 all-gather.1
where the time goes:
time: 255 us; the launch traced here: 253 us
  local copies, waits for them, and re-layouts  86.2 us (34%)
  waiting for transfers between devices  70.3 us (28%)
  matrix products  48.3 us (19%)
  other arithmetic  34.4 us (13%)
  between operations  13.7 us (5%)
    all_gather x1, waiting for transfers between devices, local(): gathered = lax.all_gather(packed, 'seq', axis=0, tiled=True)  70.3 us
    dynamic_slice x40, local copies, waits for them, and re-layouts, local(): lax.map(local_block, (queries.reshape(shape_blocks), key_rows.reshape(sha...  35.1 us
    dot_general x11, matrix products, attend_core(): jnp.einsum('hqk,khe->qhe', probs, value_set, preferred_element_type=jnp.f...  28.6 us
    reduce_sum x11, other arithmetic, attend_core(): totals = jnp.sum(expanded, axis=-1)  21.2 us
    dot_general x11, matrix products, attend_core(): jnp.einsum('qhe,khe->hqk', query_set, key_set, preferred_element_type=jnp...  19.7 us
    dynamic_update_slice x16, local copies, waits for them, and re-layouts, local(): lax.map(local_block, (queries.reshape(shape_blocks), key_rows.reshape(sha...  13.9 us
    slice x1, local copies, waits for them, and re-layouts, local(): third_level = gathered[::4]  12.3 us
    convert_element_type x1, other arithmetic, local(): put_rows(out_zero, merged.reshape(rows_one, model_width), stride, head_co...  8.06 us
  transfers between devices with their start and end apart: 1, of which 1 were waited for; matrix products, arithmetic and copies ran while one was open for 1% of the time, Pallas kernels for 0%

commit v1 on v0

v1 whole, which is shorter than its diff:
```python
import jax
import jax.numpy as jnp
from jax import lax
from jax.experimental import pallas as pl
from jax.experimental.pallas import tpu as pltpu
from jax.sharding import PartitionSpec as P

HEADS = 12
HEAD = 64
PAIR = 2 * HEAD
BLOCK = 512
HALF = BLOCK // 2
WIDTH = HEADS * HEAD
ROWS = 16
STRIDE = 256
UNIT = 2 * ROWS
VMEM = 52 << 20

MASKED = -1e30
BF16 = jnp.bfloat16
F32 = jnp.float32
TRANSPOSED = (((1,), (1,)), ((), ()))

CHUNKS = (1, 2, 4, 1)


def owner_mask(rows, row_size, columns):
    row = lax.broadcasted_iota(jnp.int32, (rows, columns), 0) // row_size
    head = lax.broadcasted_iota(jnp.int32, (rows, columns), 1) // HEAD
    return row == head


def pick_kernel(q_ref, k_ref, v_ref, q_out, kv_out):
    owned = owner_mask(ROWS, 1, WIDTH)
    for ref, out, start in ((q_ref, q_out, 0), (k_ref, kv_out, 0), (v_ref, kv_out, WIDTH)):
        rows = [
            jnp.sum(jnp.where(owned, ref[i].astype(F32), 0.0), axis=0, keepdims=True)
            for i in range(ROWS)
        ]
        out[:, start : start + WIDTH] = jnp.concatenate(rows, 0).astype(BF16)


def pick(queries, key_rows, value_rows):
    spec = pl.BlockSpec((ROWS, ROWS, WIDTH), lambda i: (0, 0, 0))
    shape = (ROWS, STRIDE, WIDTH)
    return pl.pallas_call(
        pick_kernel,
        grid=(1,),
        in_specs=[spec] * 3,
        out_specs=[
            pl.BlockSpec((ROWS, WIDTH), lambda i: (0, 0)),
            pl.BlockSpec((ROWS, 2 * WIDTH), lambda i: (0, 0)),
        ],
        out_shape=[
            jax.ShapeDtypeStruct((ROWS, WIDTH), BF16),
            jax.ShapeDtypeStruct((ROWS, 2 * WIDTH), BF16),
        ],
        compiler_params=pltpu.CompilerParams(vmem_limit_bytes=VMEM),
        name="pick",
    )(queries.reshape(shape), key_rows.reshape(shape), value_rows.reshape(shape))


def select_kernel(own_ref, one_ref, two_ref, three_ref, out_ref):
    row = lax.broadcasted_iota(jnp.int32, (UNIT, 4 * ROWS), 0)
    column = lax.broadcasted_iota(jnp.int32, (UNIT, 4 * ROWS), 1)
    source = jnp.where(
        row < 16,
        row,
        jnp.where(
            row < 24,
            16 + 2 * (row - 16),
            jnp.where(row < 28, 32 + 4 * (row - 24), 48 + 4 * (row - 28)),
        ),
    )
    chosen = (column == source).astype(BF16)
    every = jnp.concatenate([own_ref[...], one_ref[...], two_ref[...], three_ref[...]], 0)
    out_ref[...] = jnp.dot(chosen, every, preferred_element_type=F32).astype(BF16)


def select(own, one, two, three):
    return pl.pallas_call(
        select_kernel,
        out_shape=jax.ShapeDtypeStruct((UNIT, 2 * WIDTH), BF16),
        name="select",
    )(own, one, two, three)


def local_kernel(q_ref, k_ref, v_ref, *refs):
    out_ref, kept_ref = refs[-2:]
    low = lax.broadcasted_iota(jnp.int32, (1, PAIR), 1) < HEAD
    keep = lax.broadcasted_iota(jnp.int32, (HALF, HALF), 1) <= lax.broadcasted_iota(
        jnp.int32, (HALF, HALF), 0
    )

    def columns(pair):
        return slice(pair * PAIR, (pair + 1) * PAIR)

    def scores(pair):
        query = q_ref[:, columns(pair)] * jnp.asarray(HEAD**-0.5, BF16)
        key = k_ref[:, columns(pair)]
        zero = jnp.zeros_like(query)
        even, odd = jnp.where(low, query, zero), jnp.where(low, zero, query)
        early = lax.dot_general(
            jnp.concatenate([even, odd], 0), key[:HALF], TRANSPOSED, preferred_element_type=F32
        )
        late = lax.dot_general(
            jnp.concatenate([even[HALF:], odd[HALF:]], 0),
            key[HALF:],
            TRANSPOSED,
            preferred_element_type=F32,
        )
        return ((early[:BLOCK], late[:HALF]), (early[BLOCK:], late[HALF:]))

    def soften(pieces):
        results = []
        for early, late in pieces:
            first_half = jnp.where(keep, early[:HALF], MASKED)
            before = early[HALF:]
            second_half = jnp.where(keep, late, MASKED)
            top_one = jnp.max(first_half, axis=1, keepdims=True)
            top_two = jnp.max(jnp.maximum(before, second_half), axis=1, keepdims=True)
            results.append(
                (
                    jnp.exp(first_half - top_one).astype(BF16),
                    jnp.exp(before - top_two).astype(BF16),
                    jnp.exp(second_half - top_two).astype(BF16),
                    top_one,
                    top_two,
                )
            )
        return results

    def finish(pair, probs):
        value = v_ref[:, columns(pair)]
        extended = jnp.concatenate([value, jnp.ones_like(value)], 1)
        even, odd = probs
        one = jnp.dot(
            jnp.concatenate([even[0], odd[0]], 0), extended[:HALF], preferred_element_type=F32
        )
        two = jnp.dot(
            jnp.concatenate(
                [
                    jnp.concatenate([even[1], odd[1]], 0),
                    jnp.concatenate([even[2], odd[2]], 0),
                ],
                1,
            ),
            extended,
            preferred_element_type=F32,
        )
        for half, both in enumerate((one, two)):
            upper = jnp.where(low, both[:HALF, :PAIR], both[HALF:, :PAIR])
            lower = jnp.where(low, both[:HALF, PAIR:], both[HALF:, PAIR:])
            out_ref[half * HALF : (half + 1) * HALF, columns(pair)] = (upper / lower).astype(BF16)
            a, b = 2 * pair, 2 * pair + 1
            top_a = jnp.broadcast_to(even[3 + half][a : a + 1], (1, PAIR))
            top_b = jnp.broadcast_to(odd[3 + half][b : b + 1], (1, PAIR))
            for start, row in (
                (0, jnp.where(low, upper[a : a + 1], upper[b : b + 1])),
                (2, jnp.where(low, lower[a : a + 1], lower[b : b + 1])),
                (4, jnp.where(low, top_a, top_b)),
            ):
                kept_ref[start + half : start + half + 1, columns(pair)] = row

    ready = scores(0)
    for pair in range(HEADS // 2):
        later = scores(pair + 1) if pair + 1 < HEADS // 2 else None
        finish(pair, soften(ready))
        ready = later


def local_level(first, count, arrays, complete):
    spec = pl.BlockSpec((BLOCK, WIDTH), lambda i: (first + i, 0))
    operands = list(arrays)
    in_specs = [spec] * 3
    aliases = {}
    if complete is not None:
        operands.append(complete)
        in_specs.append(pl.BlockSpec(memory_space=pl.ANY))
        aliases = {3: 0}
    return pl.pallas_call(
        local_kernel,
        grid=(count,),
        in_specs=in_specs,
        out_specs=[spec, pl.BlockSpec((8, WIDTH), lambda i: (i, 0))],
        out_shape=[
            jax.ShapeDtypeStruct(arrays[0].shape, BF16),
            jax.ShapeDtypeStruct((8 * count, WIDTH), F32),
        ],
        input_output_aliases=aliases,
        compiler_params=pltpu.CompilerParams(vmem_limit_bytes=VMEM),
        cost_estimate=pl.CostEstimate(
            flops=count * HEADS * 4 * BLOCK * BLOCK * HEAD * 4,
            bytes_accessed=count * 8 * BLOCK * WIDTH,
            transcendentals=count * HEADS * BLOCK * BLOCK,
        ),
        name="local",
    )(*operands)


def merge_kernel(spot_ref, q_ref, own_ref, other_ref, *refs):
    kept_refs, old_ref, out_ref = refs[:-2], refs[-2], refs[-1]
    lanes = HEADS * ROWS
    owned = owner_mask(lanes, ROWS, WIDTH)
    query = q_ref[...] * jnp.asarray(HEAD**-0.5, BF16)
    spread = jnp.where(owned, jnp.concatenate([query] * HEADS, 0), jnp.zeros((), BF16))
    score = jnp.concatenate(
        [
            lax.dot_general(spread, ref[:, :WIDTH], TRANSPOSED, preferred_element_type=F32)
            for ref in (own_ref, other_ref)
        ],
        1,
    )
    keys = score.shape[1]
    device = spot_ref[0]
    column = lax.broadcasted_iota(jnp.int32, (1, keys), 1)
    core, x, z = column // (keys // 2), column // (4 * UNIT) % 4, column // UNIT % 4
    inner = column % UNIT
    quarter = jnp.where(inner < 16, 0, jnp.where(inner < 24, 1, jnp.where(inner < 28, 2, 3)))
    index = jnp.where(
        inner < 16, inner, jnp.where(inner < 24, 2 * (inner - 16), 4 * (inner % 4))
    )
    source = jnp.bitwise_xor(device, quarter * 32 + x * 8 + z * 2 + core)
    key_place = source * ROWS + index
    row = lax.broadcasted_iota(jnp.int32, (lanes, 1), 0) % ROWS
    query_place = device * ROWS + row
    in_one = (quarter == 0).astype(F32)
    in_two = jnp.where((quarter <= 1) & (index % 2 == 0), 1.0, 0.0)
    in_three = jnp.where(index % 4 == 0, 1.0, 0.0)
    has_two = jnp.where(row % 2 == 0, 1.0, 0.0)
    has_three = jnp.where(row % 4 == 0, 1.0, 0.0)
    count = in_one + has_two * in_two + has_three * in_three
    count = jnp.where(key_place <= query_place, count, 0.0)
    score = jnp.where(count > 0.0, score, MASKED)
    top = jnp.max(score, axis=1, keepdims=True)
    probs = jnp.exp(score - top) * count
    total = jnp.sum(probs, axis=1, keepdims=True)
    probs = probs.astype(BF16)
    result = jnp.dot(probs[:, : keys // 2], own_ref[:, WIDTH:], preferred_element_type=F32)
    result = result + jnp.dot(
        probs[:, keys // 2 :], other_ref[:, WIDTH:], preferred_element_type=F32
    )

    def gather_heads(array):
        kept = jnp.where(owned, array, 0.0)
        return jnp.sum(kept.reshape(HEADS, ROWS, WIDTH), axis=0)

    top, total, result = gather_heads(top), gather_heads(total), gather_heads(result)
    blocks = [ref[8 * i : 8 * i + 8] for ref in kept_refs for i in range(ref.shape[0] // 8)]
    result_zero, total_zero, top_zero = (
        jnp.concatenate([block[start : start + 2] for block in blocks], 0) for start in (0, 2, 4)
    )
    best = jnp.maximum(top, top_zero)
    weight, weight_zero = jnp.exp(top - best), jnp.exp(top_zero - best)
    mixed = (weight * result + weight_zero * result_zero) / (
        weight * total + weight_zero * total_zero
    )
    owned = owner_mask(ROWS, 1, WIDTH)
    for i in range(ROWS):
        out_ref[i] = jnp.where(owned, mixed[i : i + 1], old_ref[i].astype(F32)).astype(BF16)


def merge(spot, query, own, other, kept, complete):
    shape = (ROWS, STRIDE, WIDTH)
    corner = pl.BlockSpec((ROWS, ROWS, WIDTH), lambda i: (0, 0, 0))

    def whole(array):
        return pl.BlockSpec(array.shape, lambda i: (0, 0))

    merged = pl.pallas_call(
        merge_kernel,
        grid=(1,),
        in_specs=[pl.BlockSpec(memory_space=pltpu.SMEM)]
        + [whole(array) for array in (query, own, other, *kept)]
        + [corner],
        out_specs=corner,
        out_shape=jax.ShapeDtypeStruct(shape, BF16),
        input_output_aliases={4 + len(kept): 0},
        compiler_params=pltpu.CompilerParams(vmem_limit_bytes=VMEM),
        name="merge",
    )(spot, query, own, other, *kept, complete.reshape(shape))
    return merged.reshape(complete.shape)


def local(queries, key_rows, value_rows):
    devices = lax.axis_size("seq")
    arrays = (queries, key_rows, value_rows)

    def exchange(array, distance):
        return lax.ppermute(array, "seq", [(i, i ^ distance) for i in range(devices)])

    query, rows = pick(*arrays)
    complete, kept, first = None, [], 0
    stages = ((32, 64, 96), (2, 4, 6), (8, 16, 24), (1,))
    for stage, (distances, count) in enumerate(zip(stages, CHUNKS)):
        received = [exchange(rows, distance) for distance in distances]
        complete, some = local_level(first, count, arrays, complete)
        first += count
        kept.append(some)
        received, rows, complete = lax.optimization_barrier((received, rows, complete))
        if stage == 0:
            rows = select(rows, *received)
        elif stage < 3:
            rows = jnp.concatenate([rows, *received], 0)
        if stage < 3:
            rows, complete, arrays = lax.optimization_barrier((rows, complete, arrays))
    spot = lax.axis_index("seq").astype(jnp.int32).reshape(1)
    return merge(spot, query, rows, received[0], kept, complete)


def solution(mesh):
    in_specs = (P("seq", None), P("seq", None), P("seq", None))
    out_specs = P("seq", None)
    return jax.shard_map(local, mesh=mesh, in_specs=in_specs, out_specs=out_specs, check_vma=False)
```

time: 255 us -> 59.3 us (0.23)
  local copies, waits for them, and re-layouts: 86.2 us -> 1.8 us
  waiting for transfers between devices: 70.3 us -> 1.36 us
  matrix products: 48.3 us -> 0 us
  Pallas kernels: 0 us -> 41 us
  other arithmetic: 34.4 us -> 0.13 us
  starting transfers between devices: 0.01 us -> 14.7 us
  between operations: 13.7 us -> 0.09 us
    all_gather x1 -> x0, waiting for transfers between devices: 70.3 us -> none  [local(): gathered = lax.all_gather(packed, 'seq', axis=0, tiled=True)]
    dot_general x22 -> x0, matrix products: 48.3 us -> none  [the longest x11 28.6 us: attend_core(): jnp.einsum('hqk,khe->qhe', probs, value_set, preferred_element_type=jnp.f...]
    pallas_call x0 -> x7, Pallas kernels: none -> 41 us  [the longest x4 34.1 us: local_level(): pl.pallas_call(local_kernel, grid=(count,), in_specs=in_specs, out_specs=...]
    dynamic_slice x41 -> x0, local copies, waits for them, and re-layouts: 37.2 us -> none  [the longest x40 35.1 us: local(): lax.map(local_block, (queries.reshape(shape_blocks), key_rows.reshape(sha...]
    slice x13 -> x0, local copies, waits for them, and re-layouts: 28.7 us -> none  [the longest x1 12.3 us: local(): third_level = gathered[::4]]
    reduce_sum x13 -> x0, other arithmetic: 23.4 us -> none  [the longest x11 21.2 us: attend_core(): totals = jnp.sum(expanded, axis=-1)]
    dynamic_update_slice x17 -> x0, local copies, waits for them, and re-layouts: 18.6 us -> none  [the longest x16 13.9 us: local(): lax.map(local_block, (queries.reshape(shape_blocks), key_rows.reshape(sha...]
    ppermute x0 -> x10, starting transfers between devices: none -> 14.7 us  [exchange(): lax.ppermute(array, 'seq', [(i, i ^ distance) for i in range(devices)])]
  transfers between devices with their start and end apart: 1 -> 10, of which waited for: 1 -> 1; matrix products, arithmetic and copies ran while one was open for 1% -> 0% of each run, Pallas kernels for 0% -> 58%
where the time goes in v1:
time: 59.3 us; the launch traced here: 59 us
  Pallas kernels  41 us (69%)
  starting transfers between devices  14.7 us (25%)
  local copies, waits for them, and re-layouts  1.8 us (3%)
  waiting for transfers between devices  1.36 us (2%)
    pallas_call x4, Pallas kernels, local_level(): pl.pallas_call(local_kernel, grid=(count,), in_specs=in_specs, out_specs=...  34.1 us
    ppermute x10, starting transfers between devices, exchange(): lax.ppermute(array, 'seq', [(i, i ^ distance) for i in range(devices)])  14.7 us
    pallas_call x1, Pallas kernels, merge(): pl.pallas_call(merge_kernel, grid=(1,), in_specs=[pl.BlockSpec(memory_spa...  3.6 us
    unnamed x12, local copies, waits for them, and re-layouts  1.8 us
    pallas_call x1, Pallas kernels, select(): pl.pallas_call(select_kernel, out_shape=jax.ShapeDtypeStruct((UNIT, 2 * W...  1.67 us
    pallas_call x1, Pallas kernels, pick(): pl.pallas_call(pick_kernel, grid=(1,), in_specs=[spec] * 3, out_specs=[pl...  1.6 us
    ppermute x10, waiting for transfers between devices, exchange(): lax.ppermute(array, 'seq', [(i, i ^ distance) for i in range(devices)])  1.36 us
  transfers between devices with their start and end apart: 10, of which 1 were waited for; matrix products, arithmetic and copies ran while one was open for 0% of the time, Pallas kernels for 58%

profile of v1, /device:TPU:1, one launch (start us, length us, event | category | flops | bytes accessed | tf_op | source)
XLA Modules:
  0.0 59.0 jit_solution(3084820713375024438)
XLA Ops:
  0.0 1.6 %pick.1 = (bf16[16,768]{1,0:T(8,128)(2,1)S(1)}, bf16[16,1536]{1,0:T(8,128)(2,1)S(1)}) custom-call(bf16[16,256,768]{2,1,0:T(8,128)(2,1)} %bitcast.6, bf16[16,256,768]{2,1,0:T(8,128)(2,1)} %bitcast.7, bf16[16,256,768]{2,1,0:T(8,128)(2,1)} %bitcast.8), custom_call_target="tpu_custom_call" | custom-call | tf_op jit(solution)/shard_map/pick/pallas_call | solution.py:46
  1.6 3.6 %collective-permute-start.2 = (bf16[16,1536]{1,0:T(8,128)(2,1)S(1)}, bf16[16,1536]{1,0:T(8,128)(2,1)S(1)}, u32[]{:S(2)}, u32[]{:S(2)}) collective-permute-start(bf16[16,1536]{1,0:T(8,128)(2,1)S(1)} %get-tuple-element.51.own_ref), channel_id=1, source_target_pairs={{0,96},{1,97},{2,98},{3,99},{4,100},{5,101},{6,102},{7,103},{8,104... | collective-permute-start | bytes 147464 | tf_op jit(solution)/shard_map/ppermute | solution.py:290
  5.3 0.3 collective-permute-start.1
  5.6 0.3 collective-permute-start
  5.9 5.5 %local.4 = (bf16[4096,768]{1,0:T(8,128)(2,1)}, f32[8,768]{1,0:T(8,128)S(1)}) custom-call(bf16[4096,768]{1,0:T(8,128)(2,1)} %q_ref.4, bf16[4096,768]{1,0:T(8,128)(2,1)} %k_ref.4, bf16[4096,768]{1,0:T(8,128)(2,1)} %v_ref.4), custom_call_target="tpu_custom_call" | custom-call | flops 3221225472 | bytes 3145728 | tf_op jit(solution)/shard_map/local/pallas_call | solution.py:181
  11.4 0.0 collective-permute-done.2.three_ref
  11.4 0.0 collective-permute-done.1.two_ref
  11.5 0.6 copy-done.3
  12.1 0.0 copy-done.4
  12.1 0.0 copy-done.5
  12.1 1.7 %select.1 = bf16[32,1536]{1,0:T(8,128)(2,1)} custom-call(bf16[16,1536]{1,0:T(8,128)(2,1)} %copy-done, bf16[16,1536]{1,0:T(8,128)(2,1)} %copy-done.5, bf16[16,1536]{1,0:T(8,128)(2,1)} %copy-done.4, bf16[16,1536]{1,0:T(8,128)(2,1)} %copy-done.3), custom_call_target="tpu_custom_call" | custom-call | tf_op jit(solution)/shard_map/select/pallas_call | solution.py:81
  13.8 3.8 %collective-permute-start.5 = (bf16[32,1536]{1,0:T(8,128)(2,1)}, bf16[32,1536]{1,0:T(8,128)(2,1)S(1)}, u32[]{:S(2)}, u32[]{:S(2)}) collective-permute-start(bf16[32,1536]{1,0:T(8,128)(2,1)} %select.1), channel_id=1, source_target_pairs={{0,6},{1,7},{2,4},{3,5},{4,2},{5,3},{6,0},{7,1},{8,14},{9,15},{10,... | collective-permute-start | bytes 294920 | tf_op jit(solution)/shard_map/ppermute | solution.py:290
  17.5 0.6 collective-permute-start.3
  18.1 8.5 %local.5 = (bf16[4096,768]{1,0:T(8,128)(2,1)}, f32[16,768]{1,0:T(8,128)S(1)}) custom-call(bf16[4096,768]{1,0:T(8,128)(2,1)} %q_ref.4, bf16[4096,768]{1,0:T(8,128)(2,1)} %k_ref.4, bf16[4096,768]{1,0:T(8,128)(2,1)} %v_ref.4, bf16[4096,768]{1,0:T(8,128)(2,1)} %get-tuple-element.60.refs_0_), custom_call_target="tpu_custom_call", output_to_operand_aliasing={{0}: (3, {})} | custom-call | flops 6442450944 | bytes 6291456 | tf_op jit(solution)/shard_map/local/pallas_call | solution.py:181
  26.7 2.6 %collective-permute-start.8 = (bf16[128,1536]{1,0:T(8,128)(2,1)S(1)}, bf16[128,1536]{1,0:T(8,128)(2,1)S(1)}, u32[]{:S(2)}, u32[]{:S(2)}) collective-permute-start(bf16[128,1536]{1,0:T(8,128)(2,1)S(1)} %pad_maximum_fusion.1), channel_id=1, source_target_pairs={{0,24},{1,25},{2,26},{3,27},{4,28},{5,29},{6,30},{7,31},{8,16},{9,... | collective-permute-start | bytes 1179656 | tf_op jit(solution)/shard_map/ppermute | solution.py:290
  29.3 0.5 collective-permute-start.7
  29.8 0.2 collective-permute-start.6
  30.0 14.6 %local.6 = (bf16[4096,768]{1,0:T(8,128)(2,1)}, f32[32,768]{1,0:T(8,128)S(1)}) custom-call(bf16[4096,768]{1,0:T(8,128)(2,1)} %q_ref.4, bf16[4096,768]{1,0:T(8,128)(2,1)} %k_ref.4, bf16[4096,768]{1,0:T(8,128)(2,1)} %v_ref.4, bf16[4096,768]{1,0:T(8,128)(2,1)} %get-tuple-element.71.refs_0_), custom_call_target="tpu_custom_call", output_to_operand_aliasing={{0}: (3, {})} | custom-call | flops 12884901888 | bytes 12582912 | tf_op jit(solution)/shard_map/local/pallas_call | solution.py:181
  44.6 1.3 %collective-permute-done.8 = bf16[128,1536]{1,0:T(8,128)(2,1)S(1)} collective-permute-done((bf16[128,1536]{1,0:T(8,128)(2,1)S(1)}, bf16[128,1536]{1,0:T(8,128)(2,1)S(1)}, u32[]{:S(2)}, u32[]{:S(2)}) %collective-permute-start.8) | collective-permute-done | bytes 393248 | tf_op jit(solution)/shard_map/ppermute | solution.py:290
  46.0 0.1 pad_maximum_fusion.own_ref
  46.1 2.7 %collective-permute-start.9 = (bf16[512,1536]{1,0:T(8,128)(2,1)S(1)}, bf16[512,1536]{1,0:T(8,128)(2,1)S(1)}, u32[]{:S(2)}, u32[]{:S(2)}) collective-permute-start(bf16[512,1536]{1,0:T(8,128)(2,1)S(1)} %pad_maximum_fusion.own_ref), channel_id=1, source_target_pairs={{0,1},{1,0},{2,3},{3,2},{4,5},{5,4},{6,7},{7,6},{8,9},{9,8},{10,11... | collective-permute-start | bytes 4718600 | tf_op jit(solution)/shard_map/ppermute | solution.py:290
  48.8 5.5 %local.7 = (bf16[4096,768]{1,0:T(8,128)(2,1)}, f32[8,768]{1,0:T(8,128)S(1)}) custom-call(bf16[4096,768]{1,0:T(8,128)(2,1)} %q_ref.4, bf16[4096,768]{1,0:T(8,128)(2,1)} %k_ref.4, bf16[4096,768]{1,0:T(8,128)(2,1)} %v_ref.4, bf16[4096,768]{1,0:T(8,128)(2,1)} %get-tuple-element.82.refs_0_), custom_call_target="tpu_custom_call", output_to_operand_aliasing={{0}: (3, {})} | custom-call | flops 3221225472 | bytes 3145728 | tf_op jit(solution)/shard_map/local/pallas_call | solution.py:181
  54.3 1.2 %copy-done.1 = bf16[512,1536]{1,0:T(8,128)(2,1)} copy-done((bf16[512,1536]{1,0:T(8,128)(2,1)}, bf16[512,1536]{1,0:T(8,128)(2,1)S(1)}, u32[]{:S(2)}) %copy-start.1) | copy-done | bytes 1572888
  55.4 3.6 %merge.1 = bf16[16,256,768]{2,1,0:T(8,128)(2,1)} custom-call(s32[1]{0:T(128)} %bitcast.spot_ref, bf16[16,768]{1,0:T(8,128)(2,1)S(1)} %get-tuple-element.48.q_ref, bf16[512,1536]{1,0:T(8,128)(2,1)S(1)} %pad_maximum_fusion.own_ref, bf16[512,1536]{1,0:T(8,128)(2,1)} %copy-done.1, ...), custom_call_target="tpu_custom_call", output_to_operand_aliasing={{}: (8, {})} | custom-call | tf_op jit(solution)/shard_map/merge/pallas_call | solution.py:270
  (17 shorter events, 0.1 us)
Async XLA Ops:
  1.6 9.8 %copy-start = (bf16[16,1536]{1,0:T(8,128)(2,1)}, bf16[16,1536]{1,0:T(8,128)(2,1)S(1)}, u32[]{:S(2)}) copy-start(bf16[16,1536]{1,0:T(8,128)(2,1)S(1)} %get-tuple-element.51.own_ref) | copy-start | bytes 147460
  1.6 9.8 %collective-permute-start.2 = (bf16[16,1536]{1,0:T(8,128)(2,1)S(1)}, bf16[16,1536]{1,0:T(8,128)(2,1)S(1)}, u32[]{:S(2)}, u32[]{:S(2)}) collective-permute-start(bf16[16,1536]{1,0:T(8,128)(2,1)S(1)} %get-tuple-element.51.own_ref), channel_id=1, source_target_pairs={{0,96},{1,97},{2,98},{3,99},{4,100},{5,101},{6,102},{7,103},{8,104... | collective-permute-start | bytes 147464 | tf_op jit(solution)/shard_map/ppermute | solution.py:290
  5.3 6.2 %collective-permute-start.1 = (bf16[16,1536]{1,0:T(8,128)(2,1)S(1)}, bf16[16,1536]{1,0:T(8,128)(2,1)S(1)}, u32[]{:S(2)}, u32[]{:S(2)}) collective-permute-start(bf16[16,1536]{1,0:T(8,128)(2,1)S(1)} %get-tuple-element.51.own_ref), channel_id=1, source_target_pairs={{0,64},{1,65},{2,66},{3,67},{4,68},{5,69},{6,70},{7,71},{8,72},{9,... | collective-permute-start | bytes 147464 | tf_op jit(solution)/shard_map/ppermute | solution.py:290
  5.6 5.9 %collective-permute-start = (bf16[16,1536]{1,0:T(8,128)(2,1)S(1)}, bf16[16,1536]{1,0:T(8,128)(2,1)S(1)}, u32[]{:S(2)}, u32[]{:S(2)}) collective-permute-start(bf16[16,1536]{1,0:T(8,128)(2,1)S(1)} %get-tuple-element.51.own_ref), channel_id=1, source_target_pairs={{0,32},{1,33},{2,34},{3,35},{4,36},{5,37},{6,38},{7,39},{8,40},{9,... | collective-permute-start | bytes 147464 | tf_op jit(solution)/shard_map/ppermute | solution.py:290
  11.4 0.6 %copy-start.3 = (bf16[16,1536]{1,0:T(8,128)(2,1)}, bf16[16,1536]{1,0:T(8,128)(2,1)S(1)}, u32[]{:S(2)}) copy-start(bf16[16,1536]{1,0:T(8,128)(2,1)S(1)} %collective-permute-done.2.three_ref) | copy-start | bytes 147460
  11.5 0.6 %copy-start.4 = (bf16[16,1536]{1,0:T(8,128)(2,1)}, bf16[16,1536]{1,0:T(8,128)(2,1)S(1)}, u32[]{:S(2)}) copy-start(bf16[16,1536]{1,0:T(8,128)(2,1)S(1)} %collective-permute-done.1.two_ref) | copy-start | bytes 147460
  11.5 0.6 %copy-start.5 = (bf16[16,1536]{1,0:T(8,128)(2,1)}, bf16[16,1536]{1,0:T(8,128)(2,1)S(1)}, u32[]{:S(2)}) copy-start(bf16[16,1536]{1,0:T(8,128)(2,1)S(1)} %collective-permute-done.one_ref) | copy-start | bytes 147460
  13.8 12.9 %copy-start.2 = (bf16[32,1536]{1,0:T(8,128)(2,1)S(1)}, bf16[32,1536]{1,0:T(8,128)(2,1)}, u32[]{:S(2)}) copy-start(bf16[32,1536]{1,0:T(8,128)(2,1)} %select.1) | copy-start | bytes 294916
  13.8 12.9 %collective-permute-start.5 = (bf16[32,1536]{1,0:T(8,128)(2,1)}, bf16[32,1536]{1,0:T(8,128)(2,1)S(1)}, u32[]{:S(2)}, u32[]{:S(2)}) collective-permute-start(bf16[32,1536]{1,0:T(8,128)(2,1)} %select.1), channel_id=1, source_target_pairs={{0,6},{1,7},{2,4},{3,5},{4,2},{5,3},{6,0},{7,1},{8,14},{9,15},{10,... | collective-permute-start | bytes 294920 | tf_op jit(solution)/shard_map/ppermute | solution.py:290
  17.5 9.1 %collective-permute-start.4 = (bf16[32,1536]{1,0:T(8,128)(2,1)}, bf16[32,1536]{1,0:T(8,128)(2,1)S(1)}, u32[]{:S(2)}, u32[]{:S(2)}) collective-permute-start(bf16[32,1536]{1,0:T(8,128)(2,1)} %select.1), channel_id=1, source_target_pairs={{0,4},{1,5},{2,6},{3,7},{4,0},{5,1},{6,2},{7,3},{8,12},{9,13},{10,... | collective-permute-start | bytes 294920 | tf_op jit(solution)/shard_map/ppermute | solution.py:290
  17.5 9.1 %collective-permute-start.3 = (bf16[32,1536]{1,0:T(8,128)(2,1)}, bf16[32,1536]{1,0:T(8,128)(2,1)S(1)}, u32[]{:S(2)}, u32[]{:S(2)}) collective-permute-start(bf16[32,1536]{1,0:T(8,128)(2,1)} %select.1), channel_id=1, source_target_pairs={{0,2},{1,3},{2,0},{3,1},{4,6},{5,7},{6,4},{7,5},{8,10},{9,11},{10,... | collective-permute-start | bytes 294920 | tf_op jit(solution)/shard_map/ppermute | solution.py:290
  26.7 19.3 %collective-permute-start.8 = (bf16[128,1536]{1,0:T(8,128)(2,1)S(1)}, bf16[128,1536]{1,0:T(8,128)(2,1)S(1)}, u32[]{:S(2)}, u32[]{:S(2)}) collective-permute-start(bf16[128,1536]{1,0:T(8,128)(2,1)S(1)} %pad_maximum_fusion.1), channel_id=1, source_target_pairs={{0,24},{1,25},{2,26},{3,27},{4,28},{5,29},{6,30},{7,31},{8,16},{9,... | collective-permute-start | bytes 1179656 | tf_op jit(solution)/shard_map/ppermute | solution.py:290
  29.3 16.7 %collective-permute-start.7 = (bf16[128,1536]{1,0:T(8,128)(2,1)S(1)}, bf16[128,1536]{1,0:T(8,128)(2,1)S(1)}, u32[]{:S(2)}, u32[]{:S(2)}) collective-permute-start(bf16[128,1536]{1,0:T(8,128)(2,1)S(1)} %pad_maximum_fusion.1), channel_id=1, source_target_pairs={{0,16},{1,17},{2,18},{3,19},{4,20},{5,21},{6,22},{7,23},{8,24},{9,... | collective-permute-start | bytes 1179656 | tf_op jit(solution)/shard_map/ppermute | solution.py:290
  29.8 16.2 %collective-permute-start.6 = (bf16[128,1536]{1,0:T(8,128)(2,1)S(1)}, bf16[128,1536]{1,0:T(8,128)(2,1)S(1)}, u32[]{:S(2)}, u32[]{:S(2)}) collective-permute-start(bf16[128,1536]{1,0:T(8,128)(2,1)S(1)} %pad_maximum_fusion.1), channel_id=1, source_target_pairs={{0,8},{1,9},{2,10},{3,11},{4,12},{5,13},{6,14},{7,15},{8,0},{9,1},... | collective-permute-start | bytes 1179656 | tf_op jit(solution)/shard_map/ppermute | solution.py:290
  46.1 8.2 %collective-permute-start.9 = (bf16[512,1536]{1,0:T(8,128)(2,1)S(1)}, bf16[512,1536]{1,0:T(8,128)(2,1)S(1)}, u32[]{:S(2)}, u32[]{:S(2)}) collective-permute-start(bf16[512,1536]{1,0:T(8,128)(2,1)S(1)} %pad_maximum_fusion.own_ref), channel_id=1, source_target_pairs={{0,1},{1,0},{2,3},{3,2},{4,5},{5,4},{6,7},{7,6},{8,9},{9,8},{10,11... | collective-permute-start | bytes 4718600 | tf_op jit(solution)/shard_map/ppermute | solution.py:290
  54.3 1.2 %copy-start.1 = (bf16[512,1536]{1,0:T(8,128)(2,1)}, bf16[512,1536]{1,0:T(8,128)(2,1)S(1)}, u32[]{:S(2)}) copy-start(bf16[512,1536]{1,0:T(8,128)(2,1)S(1)} %collective-permute-done.9.other_ref) | copy-start | bytes 4718596

commit v2 on v1

--- a/solution.py
+++ b/solution.py
@@ -15,6 +15,8 @@
 STRIDE = 256
 UNIT = 2 * ROWS
 VMEM = 52 << 20
+LOCAL_VMEM = 52 << 20
+MERGE_VMEM = 20 << 20
 
 MASKED = -1e30
 BF16 = jnp.bfloat16
@@ -30,59 +32,44 @@
     return row == head
 
 
-def pick_kernel(q_ref, k_ref, v_ref, q_out, kv_out):
+def pick_kernel(q_ref, k_ref, v_ref, q_out, own_out, second_out, low_out, high_out):
     owned = owner_mask(ROWS, 1, WIDTH)
-    for ref, out, start in ((q_ref, q_out, 0), (k_ref, kv_out, 0), (v_ref, kv_out, WIDTH)):
-        rows = [
+
+    def diagonal(ref):
+        return [
             jnp.sum(jnp.where(owned, ref[i].astype(F32), 0.0), axis=0, keepdims=True)
             for i in range(ROWS)
         ]
-        out[:, start : start + WIDTH] = jnp.concatenate(rows, 0).astype(BF16)
+
+    def pack(rows):
+        return jnp.concatenate(rows, 0).astype(BF16)
+
+    q_out[...] = pack(diagonal(q_ref))
+    for ref, columns in ((k_ref, slice(0, WIDTH)), (v_ref, slice(WIDTH, 2 * WIDTH))):
+        rows = diagonal(ref)
+        none = [jnp.zeros_like(rows[0])] * (ROWS // 4)
+        own_out[:, columns] = pack(rows)
+        second_out[:, columns] = pack(rows[::2])
+        low_out[:, columns] = pack(rows[::4] + none)
+        high_out[:, columns] = pack(none + rows[::4])
 
 
 def pick(queries, key_rows, value_rows):
     spec = pl.BlockSpec((ROWS, ROWS, WIDTH), lambda i: (0, 0, 0))
     shape = (ROWS, STRIDE, WIDTH)
+    outs = [
+        jax.ShapeDtypeStruct(size, BF16)
+        for size in ((ROWS, WIDTH), (ROWS, 2 * WIDTH)) + ((ROWS // 2, 2 * WIDTH),) * 3
+    ]
     return pl.pallas_call(
         pick_kernel,
         grid=(1,),
         in_specs=[spec] * 3,
-        out_specs=[
-            pl.BlockSpec((ROWS, WIDTH), lambda i: (0, 0)),
-            pl.BlockSpec((ROWS, 2 * WIDTH), lambda i: (0, 0)),
-        ],
-        out_shape=[
-            jax.ShapeDtypeStruct((ROWS, WIDTH), BF16),
-            jax.ShapeDtypeStruct((ROWS, 2 * WIDTH), BF16),
-        ],
+        out_specs=[pl.BlockSpec(out.shape, lambda i: (0, 0)) for out in outs],
+        out_shape=outs,
         compiler_params=pltpu.CompilerParams(vmem_limit_bytes=VMEM),
         name="pick",
     )(queries.reshape(shape), key_rows.reshape(shape), value_rows.reshape(shape))
-
-
-def select_kernel(own_ref, one_ref, two_ref, three_ref, out_ref):
-    row = lax.broadcasted_iota(jnp.int32, (UNIT, 4 * ROWS), 0)
-    column = lax.broadcasted_iota(jnp.int32, (UNIT, 4 * ROWS), 1)
-    source = jnp.where(
-        row < 16,
-        row,
-        jnp.where(
-            row < 24,
-            16 + 2 * (row - 16),
-            jnp.where(row < 28, 32 + 4 * (row - 24), 48 + 4 * (row - 28)),
-        ),
-    )
-    chosen = (column == source).astype(BF16)
-    every = jnp.concatenate([own_ref[...], one_ref[...], two_ref[...], three_ref[...]], 0)
-    out_ref[...] = jnp.dot(chosen, every, preferred_element_type=F32).astype(BF16)
-
-
-def select(own, one, two, three):
-    return pl.pallas_call(
-        select_kernel,
-        out_shape=jax.ShapeDtypeStruct((UNIT, 2 * WIDTH), BF16),
-        name="select",
-    )(own, one, two, three)
 
 
 def local_kernel(q_ref, k_ref, v_ref, *refs):
@@ -188,7 +175,7 @@
             jax.ShapeDtypeStruct((8 * count, WIDTH), F32),
         ],
         input_output_aliases=aliases,
-        compiler_params=pltpu.CompilerParams(vmem_limit_bytes=VMEM),
+        compiler_params=pltpu.CompilerParams(vmem_limit_bytes=LOCAL_VMEM),
         cost_estimate=pl.CostEstimate(
             flops=count * HEADS * 4 * BLOCK * BLOCK * HEAD * 4,
             bytes_accessed=count * 8 * BLOCK * WIDTH,
@@ -276,7 +263,7 @@
         out_specs=corner,
         out_shape=jax.ShapeDtypeStruct(shape, BF16),
         input_output_aliases={4 + len(kept): 0},
-        compiler_params=pltpu.CompilerParams(vmem_limit_bytes=VMEM),
+        compiler_params=pltpu.CompilerParams(vmem_limit_bytes=MERGE_VMEM),
         name="merge",
     )(spot, query, own, other, *kept, complete.reshape(shape))
     return merged.reshape(complete.shape)
@@ -289,17 +276,19 @@
     def exchange(array, distance):
         return lax.ppermute(array, "seq", [(i, i ^ distance) for i in range(devices)])
 
-    query, rows = pick(*arrays)
+    query, rows, *sent = pick(*arrays)
     complete, kept, first = None, [], 0
     stages = ((32, 64, 96), (2, 4, 6), (8, 16, 24), (1,))
     for stage, (distances, count) in enumerate(zip(stages, CHUNKS)):
-        received = [exchange(rows, distance) for distance in distances]
+        if stage > 0:
+            sent = [rows] * len(distances)
+        received = [exchange(part, distance) for part, distance in zip(sent, distances)]
         complete, some = local_level(first, count, arrays, complete)
         first += count
         kept.append(some)
         received, rows, complete = lax.optimization_barrier((received, rows, complete))
         if stage == 0:
-            rows = select(rows, *received)
+            rows = jnp.concatenate([rows, received[0], received[1] + received[2]], 0)
         elif stage < 3:
             rows = jnp.concatenate([rows, *received], 0)
         if stage < 3:

time: 59.3 us -> 56 us (0.944)
  Pallas kernels: 41 us -> 38.9 us
  local copies, waits for them, and re-layouts: 1.8 us -> 0 us
  starting transfers between devices: 14.7 us -> 15.4 us
    unnamed x12 -> x0, local copies, waits for them, and re-layouts: 1.8 us -> none
    pallas_call x1 -> x0, Pallas kernels: 1.67 us -> none  [select(): pl.pallas_call(select_kernel, out_shape=jax.ShapeDtypeStruct((UNIT, 2 * W...]
    ppermute x10, starting transfers between devices: 14.7 us -> 15.4 us  [exchange(): lax.ppermute(array, 'seq', [(i, i ^ distance) for i in range(devices)])]
  transfers between devices with their start and end apart: 10 -> 10, of which waited for: 1 -> 1; matrix products, arithmetic and copies ran while one was open for 0% -> 0% of each run, Pallas kernels for 58% -> 61%
where the time goes in v2:
time: 56 us; the launch traced here: 55.8 us
  Pallas kernels  38.9 us (69%)
  starting transfers between devices  15.4 us (28%)
  waiting for transfers between devices  1.35 us (2%)
    pallas_call x4, Pallas kernels, local_level(): pl.pallas_call(local_kernel, grid=(count,), in_specs=in_specs, out_specs=...  34.1 us
    ppermute x10, starting transfers between devices, exchange(): lax.ppermute(array, 'seq', [(i, i ^ distance) for i in range(devices)])  15.4 us
    pallas_call x1, Pallas kernels, merge(): pl.pallas_call(merge_kernel, grid=(1,), in_specs=[pl.BlockSpec(memory_spa...  3.13 us
    pallas_call x1, Pallas kernels, pick(): pl.pallas_call(pick_kernel, grid=(1,), in_specs=[spec] * 3, out_specs=[pl...  1.63 us
    ppermute x10, waiting for transfers between devices, exchange(): lax.ppermute(array, 'seq', [(i, i ^ distance) for i in range(devices)])  1.35 us
  transfers between devices with their start and end apart: 10, of which 1 were waited for; matrix products, arithmetic and copies ran while one was open for 0% of the time, Pallas kernels for 61%

profile of v2, /device:TPU:1, one launch (start us, length us, event | category | flops | bytes accessed | tf_op | source)
XLA Modules:
  0.0 55.8 jit_solution(4403205048131424907)
XLA Ops:
  0.0 1.6 %pick.1 = (bf16[16,768]{1,0:T(8,128)(2,1)S(1)}, bf16[16,1536]{1,0:T(8,128)(2,1)S(1)}, bf16[8,1536]{1,0:T(8,128)(2,1)S(1)}, bf16[8,1536]{1,0:T(8,128)(2,1)S(1)}, bf16[8,1536]{1,0:T(8,128)(2,1)S(1)}) custom-call(bf16[16,256,768]{2,1,0:T(8,128)(2,1)} %bitcast.6, bf16[16,256,768]{2,1,0:T(8,128)(2,1)} %bitcast.7, bf16[16,256,768]{2,1,0:T(8,128)(2,1)} %bitcast.8), custom_call_target="tpu_custom_call" | custom-call | tf_op jit(solution)/shard_map/pick/pallas_call | solution.py:64
  1.6 2.2 %collective-permute-start = (bf16[8,1536]{1,0:T(8,128)(2,1)S(1)}, bf16[8,1536]{1,0:T(8,128)(2,1)S(1)}, u32[]{:S(2)}, u32[]{:S(2)}) collective-permute-start(bf16[8,1536]{1,0:T(8,128)(2,1)S(1)} %get-tuple-element.52), channel_id=1, source_target_pairs={{0,32},{1,33},{2,34},{3,35},{4,36},{5,37},{6,38},{7,39},{8,40},{9,... | collective-permute-start | bytes 73736 | tf_op jit(solution)/shard_map/ppermute | solution.py:277
  3.8 2.6 %collective-permute-start.1 = (bf16[8,1536]{1,0:T(8,128)(2,1)S(1)}, bf16[8,1536]{1,0:T(8,128)(2,1)S(1)}, u32[]{:S(2)}, u32[]{:S(2)}) collective-permute-start(bf16[8,1536]{1,0:T(8,128)(2,1)S(1)} %get-tuple-element.53), channel_id=1, source_target_pairs={{0,64},{1,65},{2,66},{3,67},{4,68},{5,69},{6,70},{7,71},{8,72},{9,... | collective-permute-start | bytes 73736 | tf_op jit(solution)/shard_map/ppermute | solution.py:277
  6.5 0.0 collective-permute-start.2
  6.5 5.5 %local.4 = (bf16[4096,768]{1,0:T(8,128)(2,1)}, f32[8,768]{1,0:T(8,128)S(1)}) custom-call(bf16[4096,768]{1,0:T(8,128)(2,1)} %q_ref.4, bf16[4096,768]{1,0:T(8,128)(2,1)} %k_ref.4, bf16[4096,768]{1,0:T(8,128)(2,1)} %v_ref.4), custom_call_target="tpu_custom_call" | custom-call | flops 3221225472 | bytes 3145728 | tf_op jit(solution)/shard_map/local/pallas_call | solution.py:168
  12.0 0.0 collective-permute-done
  12.0 0.0 collective-permute-done.1
  12.0 0.0 collective-permute-done.2
  12.0 3.8 %collective-permute-start.5 = (bf16[32,1536]{1,0:T(8,128)(2,1)S(1)}, bf16[32,1536]{1,0:T(8,128)(2,1)S(1)}, u32[]{:S(2)}, u32[]{:S(2)}) collective-permute-start(bf16[32,1536]{1,0:T(8,128)(2,1)S(1)} %pad_maximum_fusion.2), channel_id=1, source_target_pairs={{0,6},{1,7},{2,4},{3,5},{4,2},{5,3},{6,0},{7,1},{8,14},{9,15},{10,... | collective-permute-start | bytes 294920 | tf_op jit(solution)/shard_map/ppermute | solution.py:277
  15.9 0.0 collective-permute-start.4
  15.9 0.7 %collective-permute-start.3 = (bf16[32,1536]{1,0:T(8,128)(2,1)S(1)}, bf16[32,1536]{1,0:T(8,128)(2,1)S(1)}, u32[]{:S(2)}, u32[]{:S(2)}) collective-permute-start(bf16[32,1536]{1,0:T(8,128)(2,1)S(1)} %pad_maximum_fusion.2), channel_id=1, source_target_pairs={{0,2},{1,3},{2,0},{3,1},{4,6},{5,7},{6,4},{7,5},{8,10},{9,11},{10,... | collective-permute-start | bytes 294920 | tf_op jit(solution)/shard_map/ppermute | solution.py:277
  16.5 8.5 %local.5 = (bf16[4096,768]{1,0:T(8,128)(2,1)}, f32[16,768]{1,0:T(8,128)S(1)}) custom-call(bf16[4096,768]{1,0:T(8,128)(2,1)} %q_ref.4, bf16[4096,768]{1,0:T(8,128)(2,1)} %k_ref.4, bf16[4096,768]{1,0:T(8,128)(2,1)} %v_ref.4, bf16[4096,768]{1,0:T(8,128)(2,1)} %get-tuple-element.66.refs_0_), custom_call_target="tpu_custom_call", output_to_operand_aliasing={{0}: (3, {})} | custom-call | flops 6442450944 | bytes 6291456 | tf_op jit(solution)/shard_map/local/pallas_call | solution.py:168
  25.1 0.0 collective-permute-done.5
  25.1 0.0 collective-permute-done.4
  25.1 2.6 %collective-permute-start.8 = (bf16[128,1536]{1,0:T(8,128)(2,1)S(1)}, bf16[128,1536]{1,0:T(8,128)(2,1)S(1)}, u32[]{:S(2)}, u32[]{:S(2)}) collective-permute-start(bf16[128,1536]{1,0:T(8,128)(2,1)S(1)} %pad_maximum_fusion.1), channel_id=1, source_target_pairs={{0,24},{1,25},{2,26},{3,27},{4,28},{5,29},{6,30},{7,31},{8,16},{9,... | collective-permute-start | bytes 1179656 | tf_op jit(solution)/shard_map/ppermute | solution.py:277
  27.7 0.5 collective-permute-start.7
  28.2 0.3 collective-permute-start.6
  28.4 14.6 %local.6 = (bf16[4096,768]{1,0:T(8,128)(2,1)}, f32[32,768]{1,0:T(8,128)S(1)}) custom-call(bf16[4096,768]{1,0:T(8,128)(2,1)} %q_ref.4, bf16[4096,768]{1,0:T(8,128)(2,1)} %k_ref.4, bf16[4096,768]{1,0:T(8,128)(2,1)} %v_ref.4, bf16[4096,768]{1,0:T(8,128)(2,1)} %get-tuple-element.77.refs_0_), custom_call_target="tpu_custom_call", output_to_operand_aliasing={{0}: (3, {})} | custom-call | flops 12884901888 | bytes 12582912 | tf_op jit(solution)/shard_map/local/pallas_call | solution.py:168
  43.0 1.3 %collective-permute-done.8 = bf16[128,1536]{1,0:T(8,128)(2,1)S(1)} collective-permute-done((bf16[128,1536]{1,0:T(8,128)(2,1)S(1)}, bf16[128,1536]{1,0:T(8,128)(2,1)S(1)}, u32[]{:S(2)}, u32[]{:S(2)}) %collective-permute-start.8) | collective-permute-done | bytes 393248 | tf_op jit(solution)/shard_map/ppermute | solution.py:277
  44.4 0.1 pad_maximum_fusion.own_ref
  44.5 2.7 %collective-permute-start.9 = (bf16[512,1536]{1,0:T(8,128)(2,1)S(1)}, bf16[512,1536]{1,0:T(8,128)(2,1)S(1)}, u32[]{:S(2)}, u32[]{:S(2)}) collective-permute-start(bf16[512,1536]{1,0:T(8,128)(2,1)S(1)} %pad_maximum_fusion.own_ref), channel_id=1, source_target_pairs={{0,1},{1,0},{2,3},{3,2},{4,5},{5,4},{6,7},{7,6},{8,9},{9,8},{10,11... | collective-permute-start | bytes 4718600 | tf_op jit(solution)/shard_map/ppermute | solution.py:277
  47.2 5.5 %local.7 = (bf16[4096,768]{1,0:T(8,128)(2,1)}, f32[8,768]{1,0:T(8,128)S(1)}) custom-call(bf16[4096,768]{1,0:T(8,128)(2,1)} %q_ref.4, bf16[4096,768]{1,0:T(8,128)(2,1)} %k_ref.4, bf16[4096,768]{1,0:T(8,128)(2,1)} %v_ref.4, bf16[4096,768]{1,0:T(8,128)(2,1)} %get-tuple-element.88.refs_0_), custom_call_target="tpu_custom_call", output_to_operand_aliasing={{0}: (3, {})} | custom-call | flops 3221225472 | bytes 3145728 | tf_op jit(solution)/shard_map/local/pallas_call | solution.py:168
  52.7 0.0 collective-permute-done.9.other_ref
  52.7 3.1 %merge.1 = bf16[16,256,768]{2,1,0:T(8,128)(2,1)} custom-call(s32[1]{0:T(128)} %bitcast.spot_ref, bf16[16,768]{1,0:T(8,128)(2,1)S(1)} %get-tuple-element.51.q_ref, bf16[512,1536]{1,0:T(8,128)(2,1)S(1)} %pad_maximum_fusion.own_ref, bf16[512,1536]{1,0:T(8,128)(2,1)S(1)} %collective-permute-done.9.other_ref, ...), custom_call_target="tpu_custom_call", output_to_operand_aliasing={{}: (8, {})} | custom-call | tf_op jit(solution)/shard_map/merge/pallas_call | solution.py:257
  (6 shorter events, 0.1 us)
Async XLA Ops:
  1.6 10.3 %collective-permute-start = (bf16[8,1536]{1,0:T(8,128)(2,1)S(1)}, bf16[8,1536]{1,0:T(8,128)(2,1)S(1)}, u32[]{:S(2)}, u32[]{:S(2)}) collective-permute-start(bf16[8,1536]{1,0:T(8,128)(2,1)S(1)} %get-tuple-element.52), channel_id=1, source_target_pairs={{0,32},{1,33},{2,34},{3,35},{4,36},{5,37},{6,38},{7,39},{8,40},{9,... | collective-permute-start | bytes 73736 | tf_op jit(solution)/shard_map/ppermute | solution.py:277
  3.8 8.1 %collective-permute-start.1 = (bf16[8,1536]{1,0:T(8,128)(2,1)S(1)}, bf16[8,1536]{1,0:T(8,128)(2,1)S(1)}, u32[]{:S(2)}, u32[]{:S(2)}) collective-permute-start(bf16[8,1536]{1,0:T(8,128)(2,1)S(1)} %get-tuple-element.53), channel_id=1, source_target_pairs={{0,64},{1,65},{2,66},{3,67},{4,68},{5,69},{6,70},{7,71},{8,72},{9,... | collective-permute-start | bytes 73736 | tf_op jit(solution)/shard_map/ppermute | solution.py:277
  6.5 5.5 %collective-permute-start.2 = (bf16[8,1536]{1,0:T(8,128)(2,1)S(1)}, bf16[8,1536]{1,0:T(8,128)(2,1)S(1)}, u32[]{:S(2)}, u32[]{:S(2)}) collective-permute-start(bf16[8,1536]{1,0:T(8,128)(2,1)S(1)} %get-tuple-element.54), channel_id=1, source_target_pairs={{0,96},{1,97},{2,98},{3,99},{4,100},{5,101},{6,102},{7,103},{8,104... | collective-permute-start | bytes 73736 | tf_op jit(solution)/shard_map/ppermute | solution.py:277
  12.0 13.0 %collective-permute-start.5 = (bf16[32,1536]{1,0:T(8,128)(2,1)S(1)}, bf16[32,1536]{1,0:T(8,128)(2,1)S(1)}, u32[]{:S(2)}, u32[]{:S(2)}) collective-permute-start(bf16[32,1536]{1,0:T(8,128)(2,1)S(1)} %pad_maximum_fusion.2), channel_id=1, source_target_pairs={{0,6},{1,7},{2,4},{3,5},{4,2},{5,3},{6,0},{7,1},{8,14},{9,15},{10,... | collective-permute-start | bytes 294920 | tf_op jit(solution)/shard_map/ppermute | solution.py:277
  15.9 9.2 %collective-permute-start.4 = (bf16[32,1536]{1,0:T(8,128)(2,1)S(1)}, bf16[32,1536]{1,0:T(8,128)(2,1)S(1)}, u32[]{:S(2)}, u32[]{:S(2)}) collective-permute-start(bf16[32,1536]{1,0:T(8,128)(2,1)S(1)} %pad_maximum_fusion.2), channel_id=1, source_target_pairs={{0,4},{1,5},{2,6},{3,7},{4,0},{5,1},{6,2},{7,3},{8,12},{9,13},{10,... | collective-permute-start | bytes 294920 | tf_op jit(solution)/shard_map/ppermute | solution.py:277
  15.9 9.2 %collective-permute-start.3 = (bf16[32,1536]{1,0:T(8,128)(2,1)S(1)}, bf16[32,1536]{1,0:T(8,128)(2,1)S(1)}, u32[]{:S(2)}, u32[]{:S(2)}) collective-permute-start(bf16[32,1536]{1,0:T(8,128)(2,1)S(1)} %pad_maximum_fusion.2), channel_id=1, source_target_pairs={{0,2},{1,3},{2,0},{3,1},{4,6},{5,7},{6,4},{7,5},{8,10},{9,11},{10,... | collective-permute-start | bytes 294920 | tf_op jit(solution)/shard_map/ppermute | solution.py:277
  25.1 19.3 %collective-permute-start.8 = (bf16[128,1536]{1,0:T(8,128)(2,1)S(1)}, bf16[128,1536]{1,0:T(8,128)(2,1)S(1)}, u32[]{:S(2)}, u32[]{:S(2)}) collective-permute-start(bf16[128,1536]{1,0:T(8,128)(2,1)S(1)} %pad_maximum_fusion.1), channel_id=1, source_target_pairs={{0,24},{1,25},{2,26},{3,27},{4,28},{5,29},{6,30},{7,31},{8,16},{9,... | collective-permute-start | bytes 1179656 | tf_op jit(solution)/shard_map/ppermute | solution.py:277
  27.7 16.7 %collective-permute-start.7 = (bf16[128,1536]{1,0:T(8,128)(2,1)S(1)}, bf16[128,1536]{1,0:T(8,128)(2,1)S(1)}, u32[]{:S(2)}, u32[]{:S(2)}) collective-permute-start(bf16[128,1536]{1,0:T(8,128)(2,1)S(1)} %pad_maximum_fusion.1), channel_id=1, source_target_pairs={{0,16},{1,17},{2,18},{3,19},{4,20},{5,21},{6,22},{7,23},{8,24},{9,... | collective-permute-start | bytes 1179656 | tf_op jit(solution)/shard_map/ppermute | solution.py:277
  28.2 16.2 %collective-permute-start.6 = (bf16[128,1536]{1,0:T(8,128)(2,1)S(1)}, bf16[128,1536]{1,0:T(8,128)(2,1)S(1)}, u32[]{:S(2)}, u32[]{:S(2)}) collective-permute-start(bf16[128,1536]{1,0:T(8,128)(2,1)S(1)} %pad_maximum_fusion.1), channel_id=1, source_target_pairs={{0,8},{1,9},{2,10},{3,11},{4,12},{5,13},{6,14},{7,15},{8,0},{9,1},... | collective-permute-start | bytes 1179656 | tf_op jit(solution)/shard_map/ppermute | solution.py:277
  44.5 8.2 %collective-permute-start.9 = (bf16[512,1536]{1,0:T(8,128)(2,1)S(1)}, bf16[512,1536]{1,0:T(8,128)(2,1)S(1)}, u32[]{:S(2)}, u32[]{:S(2)}) collective-permute-start(bf16[512,1536]{1,0:T(8,128)(2,1)S(1)} %pad_maximum_fusion.own_ref), channel_id=1, source_target_pairs={{0,1},{1,0},{2,3},{3,2},{4,5},{5,4},{6,7},{7,6},{8,9},{9,8},{10,11... | collective-permute-start | bytes 4718600 | tf_op jit(solution)/shard_map/ppermute | solution.py:277
